TPU v7x, 256 devices: a whole 4x4x8 slice. The times are simulated.
256 devices in a mesh: dp: 8 (over y, core), seq: 32 (over x, z).
Axes of the slice: x: 4, y: 4, z: 8, core: 2. Of those that a mesh axis runs over, the one named last changes fastest.
Arguments:
- spatial_query: bfloat16 [8, 32, 256, 1536], P('dp', 'seq'), may hold values from -6 to 6
- spatial_key: bfloat16 [8, 32, 256, 1536], P('dp', 'seq'), may hold values from -6 to 6
- spatial_value: bfloat16 [8, 32, 256, 1536], P('dp', 'seq'), may hold values from -6 to 6
- temporal_query: bfloat16 [8, 32, 256, 1536], P('dp', 'seq'), may hold values from -6 to 6
- temporal_key: bfloat16 [8, 32, 256, 1536], P('dp', 'seq'), may hold values from -6 to 6
- out_grad: bfloat16 [8, 32, 256, 1536], P('dp', 'seq'), may hold values from -6 to 6
- segment_ids: int32 [8, 32], P('dp'), may hold values from 0 to 3, never falling along the last dimension, each value on 1 to 16 neighbouring positions
- live_counts: int32 [8, 4], P('dp'), may hold values from 64 to 192, as said below
- norm_gains: float32 [4, 128], replicated, may hold values from 0.5 to 2
Outputs:
- block_out: bfloat16 [8, 32, 256, 1536], P('dp', 'seq')
- grad_spatial_query: bfloat16 [8, 32, 256, 1536], P('dp', 'seq')
- grad_spatial_key: bfloat16 [8, 32, 256, 1536], P('dp', 'seq')
- grad_spatial_value: bfloat16 [8, 32, 256, 1536], P('dp', 'seq')
- grad_temporal_query: bfloat16 [8, 32, 256, 1536], P('dp', 'seq')
- grad_temporal_key: bfloat16 [8, 32, 256, 1536], P('dp', 'seq')
- grad_gains: float32 [4, 128], replicated
Inputs may be any that keep to these rules, and one draw needn't show every extreme that they name: `segment_ids`: segment numbers never fall along a buffer's frames; each sample holds 1 to 16 frames, and one sample of each buffer holds exactly that many. `live_counts`: every buffer has a sample with exactly 192 live positions.
All inputs are finite; a program needn't handle non-finite values.
Results may differ from a plain program's by a relative error of at most 0.03.
Values may be sent and summed in bfloat16 or wider, within the bound.
No kernel may reach another device: no remote copies, remote signals or barrier semaphores. Data moves between devices by JAX's collectives and lax.ppermute only.
A program may use at most 128 MiB of HBM per device.

v0:
```python
import math

import jax
import jax.numpy as jnp
from jax import lax
from jax.experimental import pallas as pl
from jax.experimental.pallas import tpu as pltpu
from jax.sharding import PartitionSpec as P

HD = 128
POS = 256
LIVE = 192
FEAT = 1536
SEQ = 32
DP = 8
XS = 4
ZS = 8
ROWS = LIVE // ZS
COLS = FEAT // XS
HEADS = COLS // HD
PACK_XS = 2
EPS = 1e-6
SCALE = HD ** -0.5
SCALE2 = SCALE * math.log2(math.e)
BF = jnp.bfloat16
F32 = jnp.float32


def dot_nt(a, b):
    return lax.dot_general(a, b, (((1,), (1,)), ((), ())), preferred_element_type=F32)


def dot_nn(a, b):
    return lax.dot_general(a, b, (((1,), (0,)), ((), ())), preferred_element_type=F32)


def dot_tn(a, b):
    return lax.dot_general(a, b, (((0,), (0,)), ((), ())), preferred_element_type=F32)


def unit(x):
    factor = lax.rsqrt(jnp.mean(x * x, axis=-1, keepdims=True) + EPS)
    return x * factor, factor


def unit_back(grad, hat, factor, gain):
    gd = grad * gain
    dx = factor * (gd - hat * jnp.mean(gd * hat, axis=-1, keepdims=True))
    return dx, jnp.sum(grad * hat, axis=0, keepdims=True)


def count_of(place_ref, seg_ref, counts_ref):
    return counts_ref[0, seg_ref[0, place_ref[0]]]


def spatial_weights(nq, nk, live_keys):
    e = jnp.exp2(dot_nt(nk, nq) * SCALE2)
    e = jnp.where(live_keys, e, 0.0)
    return e * (1.0 / jnp.sum(e, axis=0, keepdims=True))


def pack_kernel(
    me_ref, seg_ref, counts_ref, gains_ref, tq_ref, tk_ref, og_ref, q_ref, k_ref, v_ref, out_ref
):
    count = count_of(me_ref, seg_ref, counts_ref)
    live_rows = lax.broadcasted_iota(jnp.int32, (LIVE, HD), 0) < count
    ones = jnp.where(live_rows, 1.0, 0.0).astype(BF)
    for h in range(HEADS * PACK_XS):
        at = slice(h * HD, (h + 1) * HD)
        x, to = h // HEADS, slice(h % HEADS * HD, (h % HEADS + 1) * HD)

        def put(n, values):
            out_ref[x * ZS : (x + 1) * ZS, n, :, to] = values.reshape(ZS, ROWS, HD).astype(BF)

        put(0, tq_ref[0, 0, :, at].astype(F32))
        put(1, tk_ref[0, 0, :, at].astype(F32))
        put(2, jnp.where(live_rows, og_ref[0, 0, :, at].astype(F32), 0.0))
        qh, _ = unit(q_ref[0, 0, :, at].astype(F32))
        kh, _ = unit(k_ref[0, 0, :, at].astype(F32))
        nq = (qh * gains_ref[0:1, :]).astype(BF)
        nk = (kh * gains_ref[1:2, :]).astype(BF)
        e = jnp.exp2(dot_nt(nq, nk) * SCALE2).astype(BF)
        v = jnp.where(live_rows, v_ref[0, 0, :, at].astype(F32), 0.0).astype(BF)
        both = dot_nn(e, jnp.concatenate([v, ones], axis=1))
        put(3, jnp.where(live_rows, both[:, :HD] * (1.0 / both[:, HD:]), 0.0))


def spatial_bwd_kernel(
    place_ref, seg_ref, counts_ref, gains_ref, q_ref, k_ref, v_ref, g_ref, dq_ref, dk_ref, dv_ref, gg_ref
):
    @pl.when(pl.program_id(0) == 0)
    def _():
        gg_ref[...] = jnp.zeros_like(gg_ref)

    count = count_of(place_ref, seg_ref, counts_ref)
    live_keys = lax.broadcasted_iota(jnp.int32, (LIVE, LIVE), 0) < count
    for ref in (dq_ref, dk_ref, dv_ref):
        ref[0, 0, LIVE:, :] = jnp.zeros((POS - LIVE, COLS), BF)
    for h in range(HEADS):
        at = slice(h * HD, (h + 1) * HD)
        gq, gk = gains_ref[0:1, :], gains_ref[1:2, :]
        qh, qf = unit(q_ref[0, 0, :, at].astype(F32))
        kh, kf = unit(k_ref[0, 0, :, at].astype(F32))
        nq = (qh * gq).astype(BF)
        nk = (kh * gk).astype(BF)
        v = v_ref[0, 0, :, at]
        g = g_ref[:, :, at].astype(F32).reshape(LIVE, HD).astype(BF)
        w = spatial_weights(nq, nk, live_keys)
        dv = dot_nn(w.astype(BF), g)
        dw = dot_nt(v, g).astype(BF).astype(F32)
        ds = w * (dw - jnp.sum(dw * w, axis=0, keepdims=True))
        ds = (ds * SCALE).astype(BF)
        dnq = dot_tn(ds, nk).astype(BF).astype(F32)
        dnk = dot_nn(ds, nq).astype(BF).astype(F32)
        dq, sq = unit_back(dnq, qh, qf, gq)
        dk, sk = unit_back(dnk, kh, kf, gk)
        dq_ref[0, 0, :LIVE, at] = dq.astype(BF)
        dk_ref[0, 0, :LIVE, at] = dk.astype(BF)
        dv_ref[0, 0, :LIVE, at] = dv.astype(BF)
        gg_ref[0:1, :] += sq
        gg_ref[1:2, :] += sk


def cut(a, j):
    return a[:, 8 * j : 8 * j + 8, :].reshape(SEQ * 8, HD)


def paste(parts):
    return jnp.concatenate([a.reshape(SEQ, 8, HD) for a in parts], axis=1).astype(BF)


def temporal_weights(qh, kh, gq, gk, mask):
    nq = (qh * gq).astype(BF)
    nk = (kh * gk).astype(BF)
    e = jnp.exp2(dot_nt(nk, nq) * SCALE2) * mask
    return nq, nk, e * (1.0 / jnp.sum(e, axis=0, keepdims=True))


def temporal_value_kernel(gains_ref, mask_ref, got_ref, out_ref):
    gq, gk = gains_ref[2:3, :], gains_ref[3:4, :]
    mask = mask_ref[...]
    for h in range(HEADS):
        at = slice(h * HD, (h + 1) * HD)
        tq, tk, og = [got_ref[:, n, :, at].astype(F32) for n in range(3)]
        parts = []
        for j in range(ROWS // 8):
            qh, _ = unit(cut(tq, j))
            kh, _ = unit(cut(tk, j))
            _, _, w = temporal_weights(qh, kh, gq, gk, mask)
            parts.append(dot_nn(w.astype(BF), cut(og, j).astype(BF)))
        out_ref[:, :, at] = paste(parts)


def temporal_kernel(gains_ref, mask_ref, tq_ref, tk_ref, og_ref, so_ref, out_ref, gg_ref):
    @pl.when(pl.program_id(0) == 0)
    def _():
        gg_ref[...] = jnp.zeros_like(gg_ref)

    gq, gk = gains_ref[2:3, :], gains_ref[3:4, :]
    mask = mask_ref[...]
    tq, tk, og, so = [ref[:, 0].astype(F32) for ref in (tq_ref, tk_ref, og_ref, so_ref)]
    parts = []
    for j in range(ROWS // 8):
        qh, qf = unit(cut(tq, j))
        kh, kf = unit(cut(tk, j))
        g = cut(og, j).astype(BF)
        v = cut(so, j).astype(BF)
        nq, nk, w = temporal_weights(qh, kh, gq, gk, mask)
        o = dot_tn(w.astype(BF), v)
        dw = dot_nt(v, g).astype(BF).astype(F32)
        ds = w * (dw - jnp.sum(dw * w, axis=0, keepdims=True))
        ds = (ds * SCALE).astype(BF)
        dnq = dot_tn(ds, nk).astype(BF).astype(F32)
        dnk = dot_nn(ds, nq).astype(BF).astype(F32)
        dq, sq = unit_back(dnq, qh, qf, gq)
        dk, sk = unit_back(dnk, kh, kf, gk)
        gg_ref[0:1, :] += sq
        gg_ref[1:2, :] += sk
        parts.append([o, dq, dk])
    for n, array in enumerate(zip(*parts)):
        out_ref[:, n] = paste(array)


def finish_kernel(*refs):
    n = len(refs) // 2
    for src, dst in zip(refs[:n], refs[n:]):
        dst[0, 0, LIVE:, :] = jnp.zeros((POS - LIVE, FEAT), BF)
        for x in range(XS):
            part = src[x * ZS : (x + 1) * ZS, 0].astype(F32).reshape(LIVE, COLS)
            dst[0, 0, :LIVE, x * COLS : (x + 1) * COLS] = part.astype(BF)


SMEM = pl.BlockSpec(memory_space=pltpu.SMEM)
PARAMS = pltpu.CompilerParams(vmem_limit_bytes=32 << 20)
WIDE = pltpu.CompilerParams(vmem_limit_bytes=60 << 20)


def cost(flops, arrays):
    return pl.CostEstimate(flops=flops, bytes_accessed=arrays * 2 * LIVE * FEAT, transcendentals=0)


def exchange(values):
    return lax.all_to_all(values, "seq", split_axis=0, concat_axis=0, tiled=True)


def flips(values, axis, masks):
    size = lax.axis_size(axis)
    return [lax.ppermute(values, axis, [(i, i ^ mask) for i in range(size)]) for mask in masks]


def add_flips(values, axis, a, b):
    one, two, both = flips(values, axis, (a, b, a ^ b))
    return (values + one) + (two + both)


def live_block():
    return pl.BlockSpec((1, 1, LIVE, COLS), lambda i: (0, 0, 0, i))


def full_block():
    return pl.BlockSpec((1, 1, POS, COLS), lambda i: (0, 0, 0, i))


def finish(packed, places):
    full = jax.ShapeDtypeStruct((1, 1, POS, FEAT), BF)
    return pl.pallas_call(
        finish_kernel,
        name="finish",
        grid=(1,),
        out_shape=[full] * len(places),
        in_specs=[
            pl.BlockSpec((SEQ, 1, ROWS, COLS), lambda i, n=n: (0, n, 0, 0)) for n in places
        ],
        out_specs=[pl.BlockSpec((1, 1, POS, FEAT), lambda i: (0, 0, 0, 0))] * len(places),
        compiler_params=PARAMS,
        cost_estimate=cost(0, 2 * len(places)),
    )(*[packed] * len(places))


def per_device(sq, sk, sv, tq, tk, og, segment_ids, live_counts, norm_gains):
    me = lax.axis_index("seq").astype(jnp.int32).reshape(1)
    places = (me, segment_ids, live_counts)
    full = jax.ShapeDtypeStruct((1, 1, POS, FEAT), BF)
    packed = jax.ShapeDtypeStruct((SEQ, ROWS, COLS), BF)
    packed3 = jax.ShapeDtypeStruct((SEQ, 3, ROWS, COLS), BF)
    gains_spec = pl.BlockSpec((4, HD), lambda i: (0, 0))
    gg_spec = pl.BlockSpec((2, HD), lambda i: (0, 0))
    gg_shape = jax.ShapeDtypeStruct((2, HD), F32)

    sent = pl.pallas_call(
        pack_kernel,
        name="pack",
        grid=(XS // PACK_XS,),
        out_shape=jax.ShapeDtypeStruct((SEQ, 4, ROWS, COLS), BF),
        in_specs=[SMEM] * 3
        + [gains_spec]
        + [pl.BlockSpec((1, 1, LIVE, PACK_XS * COLS), lambda i: (0, 0, 0, i))] * 6,
        out_specs=pl.BlockSpec((PACK_XS * ZS, 4, ROWS, COLS), lambda i: (i, 0, 0, 0)),
        compiler_params=WIDE,
        cost_estimate=cost(4 * LIVE * LIVE * FEAT, 10),
    )(*places, norm_gains, tq, tk, og, sq, sk, sv)
    got = exchange(sent)

    seg = jnp.repeat(segment_ids[0], 8)
    pos = jnp.arange(SEQ * 8, dtype=jnp.int32) % 8
    mask = (seg[:, None] == seg[None, :]) & (pos[:, None] == pos[None, :])
    got, mask = lax.optimization_barrier((got, mask.astype(F32)))

    def part(n):
        return pl.BlockSpec((SEQ, 1, ROWS, HD), lambda i: (0, n, 0, i))

    temporal_in = [gains_spec, pl.BlockSpec((SEQ * 8, SEQ * 8), lambda i: (0, 0))]
    temporal_in += [part(n) for n in range(4)]
    whole = pl.BlockSpec(memory_space=pltpu.VMEM)
    dso = pl.pallas_call(
        temporal_value_kernel,
        name="temporal_value",
        out_shape=packed,
        in_specs=[whole] * 3,
        out_specs=whole,
        compiler_params=PARAMS,
        cost_estimate=cost(4 * 9 * 256 * 256 * HD, 4),
    )(norm_gains, mask, got)
    got, dso = lax.optimization_barrier((got, dso))
    dso = exchange(dso)

    back, gains_t = pl.pallas_call(
        temporal_kernel,
        name="temporal",
        grid=(HEADS,),
        out_shape=[packed3, gg_shape],
        in_specs=temporal_in,
        out_specs=[pl.BlockSpec((SEQ, 3, ROWS, HD), lambda i: (0, 0, 0, i)), gg_spec],
        compiler_params=PARAMS,
        cost_estimate=cost(12 * 9 * 256 * 256 * HD, 7),
    )(norm_gains, mask, got, got, got, got)
    back, dso = lax.optimization_barrier((back, dso))
    back = exchange(back)

    dsq, dsk, dsv, gains_s = pl.pallas_call(
        spatial_bwd_kernel,
        name="spatial_bwd",
        grid=(XS,),
        out_shape=[full, full, full, gg_shape],
        in_specs=[SMEM] * 3 + [gains_spec] + [live_block()] * 3 + [pl.BlockSpec((ZS, ROWS, COLS), lambda i: (i, 0, 0))],
        out_specs=[full_block()] * 3 + [gg_spec],
        compiler_params=PARAMS,
        cost_estimate=cost(14 * LIVE * LIVE * FEAT, 8),
    )(*places, norm_gains, sq, sk, sv, dso)
    gains = jnp.concatenate([gains_s, gains_t], axis=0)
    gains = gains + flips(gains, "dp", (1,))[0]
    gains = add_flips(gains, "dp", 2, 4)
    gains = add_flips(gains, "seq", 8, 16)
    gains = add_flips(gains, "seq", 2, 4)
    gains, back = lax.optimization_barrier((gains, back))
    gains = gains + flips(gains, "seq", (1,))[0]
    o, dtq, dtk = finish(back, [0, 1, 2])
    return o, dsq, dsk, dsv, dtq, dtk, gains


def solution(mesh):
    big = P("dp", "seq", None, None)
    return jax.shard_map(
        per_device,
        mesh=mesh,
        in_specs=(big,) * 6 + (P("dp", None), P("dp", None), P()),
        out_specs=(big,) * 6 + (P(),),
        check_vma=False,
    )
```

profile of v0, /device:TPU:12, one launch (start us, length us, event | category | flops | bytes accessed | tf_op | source)
XLA Modules:
  0.0 151.4 jit_solution(17018829333225797990)
XLA Ops:
  0.6 4.3 %pack.1 = bf16[32,4,24,384]{3,2,1,0:T(8,128)(2,1)} custom-call(s32[1]{0:T(128)} %bitcast.me_ref.place_ref, s32[1,32]{1,0:T(1,128)} %seg_ref.3, s32[1,4]{1,0:T(1,128)} %counts_ref.3, f32[4,128]{1,0:T(4,128)} %gains_ref.7, bf16[1,1,256,1536]{3,2,1,0:T(8,128)(2,1)} %tq_ref.1, bf16[1,1,256,1536]{3,2,1,0:T(8,128)(2,1)} %tk_ref.1, ...), custom_call_target="tpu_custom_call" | custom-call | flops 226492416 | bytes 5898240 | tf_op jit(solution)/shard_map/pack/pallas_call | solution.py:250
  4.9 0.0 copy-start.5
  4.9 0.0 copy-start.4
  4.9 11.7 %all-to-all-start = ((bf16[32,4,24,384]{3,2,1,0:T(8,128)(2,1)}), bf16[32,4,24,384]{3,2,1,0:T(8,128)(2,1)S(1)}, u32[]{:S(2)}, u32[]{:S(2)}) async-start(bf16[32,4,24,384]{3,2,1,0:T(8,128)(2,1)} %pack.1), calls=%async_computation | async-start | bytes 4718592 | tf_op jit(solution)/shard_map/all_to_all | solution.py:203
  16.7 0.0 copy-done.5
  16.7 0.1 broadcast_in_dim.2
  16.7 0.1 eq.30
  16.8 0.1 and_convert_fusion.mask_ref
  17.0 53.7 %all-to-all-done.got_ref.tq_ref.tk_ref.og_ref.so_ref = bf16[32,4,24,384]{3,2,1,0:T(8,128)(2,1)S(1)} async-done(((bf16[32,4,24,384]{3,2,1,0:T(8,128)(2,1)}), bf16[32,4,24,384]{3,2,1,0:T(8,128)(2,1)S(1)}, u32[]{:S(2)}, u32[]{:S(2)}) %all-to-all-start) | async-done | bytes 2359328 | tf_op jit(solution)/shard_map/all_to_all | solution.py:203
  70.7 0.0 copy-done.4
  70.7 2.3 %temporal_value.1 = bf16[32,24,384]{2,1,0:T(8,128)(2,1)} custom-call(f32[4,128]{1,0:T(4,128)S(1)} %copy-done.4, f32[256,256]{1,0:T(8,128)S(1)} %and_convert_fusion.mask_ref, bf16[32,4,24,384]{3,2,1,0:T(8,128)(2,1)S(1)} %all-to-all-done.got_ref.tq_ref.tk_ref.og_ref.so_ref), custom_call_target="tpu_custom_call" | custom-call | flops 301989888 | bytes 2359296 | tf_op jit(solution)/shard_map/temporal_value/pallas_call | solution.py:275
  73.0 7.8 %all-to-all-start.1 = ((bf16[32,24,384]{2,1,0:T(8,128)(2,1)}), bf16[32,24,384]{2,1,0:T(8,128)(2,1)}, u32[]{:S(2)}, u32[]{:S(2)}) async-start(bf16[32,24,384]{2,1,0:T(8,128)(2,1)} %temporal_value.1), calls=%async_computation.1 | async-start | bytes 1179648 | tf_op jit(solution)/shard_map/all_to_all | solution.py:203
  80.8 6.5 %temporal.1 = (bf16[32,3,24,384]{3,2,1,0:T(8,128)(2,1)S(1)}, f32[2,128]{1,0:T(2,128)S(1)}) custom-call(f32[4,128]{1,0:T(4,128)S(1)} %copy-done.4, f32[256,256]{1,0:T(8,128)S(1)} %and_convert_fusion.mask_ref, bf16[32,4,24,384]{3,2,1,0:T(8,128)(2,1)S(1)} %all-to-all-done.got_ref.tq_ref.tk_ref.og_ref.so_ref, ...), custom_call_target="tpu_custom_call" | custom-call | flops 905969664 | bytes 4128768 | tf_op jit(solution)/shard_map/temporal/pallas_call | solution.py:287
  87.3 0.0 copy-start.3
  87.3 1.2 copy-done.3
  88.6 8.6 %all-to-all-done.1.g_ref = bf16[32,24,384]{2,1,0:T(8,128)(2,1)} async-done(((bf16[32,24,384]{2,1,0:T(8,128)(2,1)}), bf16[32,24,384]{2,1,0:T(8,128)(2,1)}, u32[]{:S(2)}, u32[]{:S(2)}) %all-to-all-start.1) | async-done | bytes 589856 | tf_op jit(solution)/shard_map/all_to_all | solution.py:203
  97.1 7.5 %all-to-all-start.2 = ((bf16[32,3,24,384]{3,2,1,0:T(8,128)(2,1)}), bf16[32,3,24,384]{3,2,1,0:T(8,128)(2,1)S(1)}, u32[]{:S(2)}, u32[]{:S(2)}) async-start(bf16[32,3,24,384]{3,2,1,0:T(8,128)(2,1)} %copy-done.3), calls=%async_computation.2 | async-start | bytes 3538944 | tf_op jit(solution)/shard_map/all_to_all | solution.py:203
  104.7 0.0 copy-done
  104.7 0.0 copy-done.1
  104.7 0.0 copy-done.6
  104.7 0.0 copy-start.2
  104.7 1.1 copy-done.2
  105.8 8.6 %spatial_bwd.1 = (bf16[1,1,256,1536]{3,2,1,0:T(8,128)(2,1)}, bf16[1,1,256,1536]{3,2,1,0:T(8,128)(2,1)}, bf16[1,1,256,1536]{3,2,1,0:T(8,128)(2,1)}, f32[2,128]{1,0:T(2,128)S(1)}) custom-call(s32[1]{0:T(128)} %bitcast.me_ref.place_ref, s32[1,32]{1,0:T(1,128)S(1)} %copy-done.5, s32[1,4]{1,0:T(1,128)S(1)} %copy-done.6, f32[4,128]{1,0:T(4,128)S(1)} %copy-done.4, ...), custom_call_target="tpu_custom_call" | custom-call | flops 792723456 | bytes 4718592 | tf_op jit(solution)/shard_map/spatial_bwd/pallas_call | solution.py:300
  114.4 0.1 collective-permute-start
  114.5 1.1 collective-permute-done
  115.7 1.7 %collective-permute-start.3 = (f32[4,128]{1,0:T(4,128)S(1)}, f32[4,128]{1,0:T(4,128)S(1)}, u32[]{:S(2)}, u32[]{:S(2)}) collective-permute-start(f32[4,128]{1,0:T(4,128)S(1)} %fusion), channel_id=1, source_target_pairs={{0,192},{32,224},{64,128},{96,160},{128,64},{160,96},{192,0},{224,... | collective-permute-start | bytes 6152 | tf_op jit(solution)/shard_map/ppermute | solution.py:208
  117.3 0.9 collective-permute-start.2
  118.3 1.6 %collective-permute-start.1 = (f32[4,128]{1,0:T(4,128)S(1)}, f32[4,128]{1,0:T(4,128)S(1)}, u32[]{:S(2)}, u32[]{:S(2)}) collective-permute-start(f32[4,128]{1,0:T(4,128)S(1)} %fusion), channel_id=1, source_target_pairs={{0,64},{32,96},{64,0},{96,32},{128,192},{160,224},{192,128},{224,1... | collective-permute-start | bytes 6152 | tf_op jit(solution)/shard_map/ppermute | solution.py:208
  119.8 0.0 collective-permute-done.3
  119.9 2.6 %collective-permute-done.2 = f32[4,128]{1,0:T(4,128)S(1)} collective-permute-done((f32[4,128]{1,0:T(4,128)S(1)}, f32[4,128]{1,0:T(4,128)S(1)}, u32[]{:S(2)}, u32[]{:S(2)}) %collective-permute-start.2) | collective-permute-done | bytes 2080 | tf_op jit(solution)/shard_map/ppermute | solution.py:208
  122.4 0.0 collective-permute-done.1
  122.4 0.6 collective-permute-start.6
  123.1 2.7 %collective-permute-start.5 = (f32[4,128]{1,0:T(4,128)S(1)}, f32[4,128]{1,0:T(4,128)S(1)}, u32[]{:S(2)}, u32[]{:S(2)}) collective-permute-start(f32[4,128]{1,0:T(4,128)S(1)} %add_add_fusion.2), channel_id=1, source_target_pairs={{0,16},{1,17},{2,18},{3,19},{4,20},{5,21},{6,22},{7,23},{8,24},{9,... | collective-permute-start | bytes 6152 | tf_op jit(solution)/shard_map/ppermute | solution.py:208
  125.8 0.8 collective-permute-start.4
  126.6 0.0 collective-permute-done.6
  126.6 1.6 %collective-permute-done.5 = f32[4,128]{1,0:T(4,128)S(1)} collective-permute-done((f32[4,128]{1,0:T(4,128)S(1)}, f32[4,128]{1,0:T(4,128)S(1)}, u32[]{:S(2)}, u32[]{:S(2)}) %collective-permute-start.5) | collective-permute-done | bytes 2080 | tf_op jit(solution)/shard_map/ppermute | solution.py:208
  128.2 1.2 collective-permute-done.4
  129.4 3.8 %collective-permute-start.9 = (f32[4,128]{1,0:T(4,128)S(1)}, f32[4,128]{1,0:T(4,128)S(1)}, u32[]{:S(2)}, u32[]{:S(2)}) collective-permute-start(f32[4,128]{1,0:T(4,128)S(1)} %add_add_fusion.1), channel_id=1, source_target_pairs={{0,6},{1,7},{2,4},{3,5},{4,2},{5,3},{6,0},{7,1},{8,14},{9,15},{10,... | collective-permute-start | bytes 6152 | tf_op jit(solution)/shard_map/ppermute | solution.py:208
  133.2 2.1 %collective-permute-start.8 = (f32[4,128]{1,0:T(4,128)S(1)}, f32[4,128]{1,0:T(4,128)S(1)}, u32[]{:S(2)}, u32[]{:S(2)}) collective-permute-start(f32[4,128]{1,0:T(4,128)S(1)} %add_add_fusion.1), channel_id=1, source_target_pairs={{0,4},{1,5},{2,6},{3,7},{4,0},{5,1},{6,2},{7,3},{8,12},{9,13},{10,... | collective-permute-start | bytes 6152 | tf_op jit(solution)/shard_map/ppermute | solution.py:208
  135.3 0.6 collective-permute-start.7
  135.9 9.3 %collective-permute-done.9 = f32[4,128]{1,0:T(4,128)S(1)} collective-permute-done((f32[4,128]{1,0:T(4,128)S(1)}, f32[4,128]{1,0:T(4,128)S(1)}, u32[]{:S(2)}, u32[]{:S(2)}) %collective-permute-start.9) | collective-permute-done | bytes 2080 | tf_op jit(solution)/shard_map/ppermute | solution.py:208
  145.2 1.9 %collective-permute-done.8 = f32[4,128]{1,0:T(4,128)S(1)} collective-permute-done((f32[4,128]{1,0:T(4,128)S(1)}, f32[4,128]{1,0:T(4,128)S(1)}, u32[]{:S(2)}, u32[]{:S(2)}) %collective-permute-start.8) | collective-permute-done | bytes 2080 | tf_op jit(solution)/shard_map/ppermute | solution.py:208
  147.1 0.0 collective-permute-done.7
  147.1 0.0 all-to-all-done.2.refs_0_.refs_1_.refs_2_
  147.2 1.2 collective-permute-start.10
  148.3 1.5 %finish.1 = (bf16[1,1,256,1536]{3,2,1,0:T(8,128)(2,1)}, bf16[1,1,256,1536]{3,2,1,0:T(8,128)(2,1)}, bf16[1,1,256,1536]{3,2,1,0:T(8,128)(2,1)}) custom-call(bf16[32,3,24,384]{3,2,1,0:T(8,128)(2,1)S(1)} %all-to-all-done.2.refs_0_.refs_1_.refs_2_, bf16[32,3,24,384]{3,2,1,0:T(8,128)(2,1)S(1)} %all-to-all-done.2.refs_0_.refs_1_.refs_2_, ...), custom_call_target="tpu_custom_call" | custom-call | bytes 3538944 | tf_op jit(solution)/shard_map/finish/pallas_call | solution.py:226
  149.8 1.0 collective-permute-done.10
  150.8 0.6 add.58
  (9 shorter events, 0.0 us)
Async XLA Ops:
  4.9 11.8 %copy-start.5 = (s32[1,32]{1,0:T(1,128)S(1)}, s32[1,32]{1,0:T(1,128)}, u32[]{:S(2)}) copy-start(s32[1,32]{1,0:T(1,128)} %seg_ref.3) | copy-start | bytes 388
  4.9 65.8 %copy-start.4 = (f32[4,128]{1,0:T(4,128)S(1)}, f32[4,128]{1,0:T(4,128)}, u32[]{:S(2)}) copy-start(f32[4,128]{1,0:T(4,128)} %gains_ref.7) | copy-start | bytes 6148
  4.9 65.8 %all-to-all-start = ((bf16[32,4,24,384]{3,2,1,0:T(8,128)(2,1)}), bf16[32,4,24,384]{3,2,1,0:T(8,128)(2,1)S(1)}, u32[]{:S(2)}, u32[]{:S(2)}) async-start(bf16[32,4,24,384]{3,2,1,0:T(8,128)(2,1)} %pack.1), calls=%async_computation | async-start | bytes 4718592 | tf_op jit(solution)/shard_map/all_to_all | solution.py:203
  73.0 24.1 %all-to-all-start.1 = ((bf16[32,24,384]{2,1,0:T(8,128)(2,1)}), bf16[32,24,384]{2,1,0:T(8,128)(2,1)}, u32[]{:S(2)}, u32[]{:S(2)}) async-start(bf16[32,24,384]{2,1,0:T(8,128)(2,1)} %temporal_value.1), calls=%async_computation.1 | async-start | bytes 1179648 | tf_op jit(solution)/shard_map/all_to_all | solution.py:203
  87.3 1.3 copy-start.3
  88.6 16.1 %copy-start = (bf16[1,1,256,1536]{3,2,1,0:T(8,128)(2,1)S(1)}, bf16[1,1,256,1536]{3,2,1,0:T(8,128)(2,1)}, u32[]{:S(2)}) copy-start(bf16[1,1,256,1536]{3,2,1,0:T(8,128)(2,1)} %q_ref.3) | copy-start | bytes 2359300
  88.6 16.1 %copy-start.1 = (bf16[1,1,256,1536]{3,2,1,0:T(8,128)(2,1)S(1)}, bf16[1,1,256,1536]{3,2,1,0:T(8,128)(2,1)}, u32[]{:S(2)}) copy-start(bf16[1,1,256,1536]{3,2,1,0:T(8,128)(2,1)} %k_ref.3) | copy-start | bytes 2359300
  88.6 16.1 %copy-start.6 = (s32[1,4]{1,0:T(1,128)S(1)}, s32[1,4]{1,0:T(1,128)}, u32[]{:S(2)}) copy-start(s32[1,4]{1,0:T(1,128)} %counts_ref.3) | copy-start | bytes 52
  97.1 50.0 %all-to-all-start.2 = ((bf16[32,3,24,384]{3,2,1,0:T(8,128)(2,1)}), bf16[32,3,24,384]{3,2,1,0:T(8,128)(2,1)S(1)}, u32[]{:S(2)}, u32[]{:S(2)}) async-start(bf16[32,3,24,384]{3,2,1,0:T(8,128)(2,1)} %copy-done.3), calls=%async_computation.2 | async-start | bytes 3538944 | tf_op jit(solution)/shard_map/all_to_all | solution.py:203
  104.7 1.1 copy-start.2
  114.4 1.2 collective-permute-start
  115.7 4.2 %collective-permute-start.3 = (f32[4,128]{1,0:T(4,128)S(1)}, f32[4,128]{1,0:T(4,128)S(1)}, u32[]{:S(2)}, u32[]{:S(2)}) collective-permute-start(f32[4,128]{1,0:T(4,128)S(1)} %fusion), channel_id=1, source_target_pairs={{0,192},{32,224},{64,128},{96,160},{128,64},{160,96},{192,0},{224,... | collective-permute-start | bytes 6152 | tf_op jit(solution)/shard_map/ppermute | solution.py:208
  117.3 5.1 %collective-permute-start.2 = (f32[4,128]{1,0:T(4,128)S(1)}, f32[4,128]{1,0:T(4,128)S(1)}, u32[]{:S(2)}, u32[]{:S(2)}) collective-permute-start(f32[4,128]{1,0:T(4,128)S(1)} %fusion), channel_id=1, source_target_pairs={{0,128},{32,160},{64,192},{96,224},{128,0},{160,32},{192,64},{224,... | collective-permute-start | bytes 6152 | tf_op jit(solution)/shard_map/ppermute | solution.py:208
  118.3 4.2 %collective-permute-start.1 = (f32[4,128]{1,0:T(4,128)S(1)}, f32[4,128]{1,0:T(4,128)S(1)}, u32[]{:S(2)}, u32[]{:S(2)}) collective-permute-start(f32[4,128]{1,0:T(4,128)S(1)} %fusion), channel_id=1, source_target_pairs={{0,64},{32,96},{64,0},{96,32},{128,192},{160,224},{192,128},{224,1... | collective-permute-start | bytes 6152 | tf_op jit(solution)/shard_map/ppermute | solution.py:208
  122.4 4.2 %collective-permute-start.6 = (f32[4,128]{1,0:T(4,128)S(1)}, f32[4,128]{1,0:T(4,128)S(1)}, u32[]{:S(2)}, u32[]{:S(2)}) collective-permute-start(f32[4,128]{1,0:T(4,128)S(1)} %add_add_fusion.2), channel_id=1, source_target_pairs={{0,24},{1,25},{2,26},{3,27},{4,28},{5,29},{6,30},{7,31},{8,16},{9,... | collective-permute-start | bytes 6152 | tf_op jit(solution)/shard_map/ppermute | solution.py:208
  123.1 5.1 %collective-permute-start.5 = (f32[4,128]{1,0:T(4,128)S(1)}, f32[4,128]{1,0:T(4,128)S(1)}, u32[]{:S(2)}, u32[]{:S(2)}) collective-permute-start(f32[4,128]{1,0:T(4,128)S(1)} %add_add_fusion.2), channel_id=1, source_target_pairs={{0,16},{1,17},{2,18},{3,19},{4,20},{5,21},{6,22},{7,23},{8,24},{9,... | collective-permute-start | bytes 6152 | tf_op jit(solution)/shard_map/ppermute | solution.py:208
  125.8 3.6 %collective-permute-start.4 = (f32[4,128]{1,0:T(4,128)S(1)}, f32[4,128]{1,0:T(4,128)S(1)}, u32[]{:S(2)}, u32[]{:S(2)}) collective-permute-start(f32[4,128]{1,0:T(4,128)S(1)} %add_add_fusion.2), channel_id=1, source_target_pairs={{0,8},{1,9},{2,10},{3,11},{4,12},{5,13},{6,14},{7,15},{8,0},{9,1},... | collective-permute-start | bytes 6152 | tf_op jit(solution)/shard_map/ppermute | solution.py:208
  129.4 15.8 %collective-permute-start.9 = (f32[4,128]{1,0:T(4,128)S(1)}, f32[4,128]{1,0:T(4,128)S(1)}, u32[]{:S(2)}, u32[]{:S(2)}) collective-permute-start(f32[4,128]{1,0:T(4,128)S(1)} %add_add_fusion.1), channel_id=1, source_target_pairs={{0,6},{1,7},{2,4},{3,5},{4,2},{5,3},{6,0},{7,1},{8,14},{9,15},{10,... | collective-permute-start | bytes 6152 | tf_op jit(solution)/shard_map/ppermute | solution.py:208
  133.2 13.9 %collective-permute-start.8 = (f32[4,128]{1,0:T(4,128)S(1)}, f32[4,128]{1,0:T(4,128)S(1)}, u32[]{:S(2)}, u32[]{:S(2)}) collective-permute-start(f32[4,128]{1,0:T(4,128)S(1)} %add_add_fusion.1), channel_id=1, source_target_pairs={{0,4},{1,5},{2,6},{3,7},{4,0},{5,1},{6,2},{7,3},{8,12},{9,13},{10,... | collective-permute-start | bytes 6152 | tf_op jit(solution)/shard_map/ppermute | solution.py:208
  135.3 11.8 %collective-permute-start.7 = (f32[4,128]{1,0:T(4,128)S(1)}, f32[4,128]{1,0:T(4,128)S(1)}, u32[]{:S(2)}, u32[]{:S(2)}) collective-permute-start(f32[4,128]{1,0:T(4,128)S(1)} %add_add_fusion.1), channel_id=1, source_target_pairs={{0,2},{1,3},{2,0},{3,1},{4,6},{5,7},{6,4},{7,5},{8,10},{9,11},{10,... | collective-permute-start | bytes 6152 | tf_op jit(solution)/shard_map/ppermute | solution.py:208
  147.2 3.7 %collective-permute-start.10 = (f32[4,128]{1,0:T(4,128)S(1)}, f32[4,128]{1,0:T(4,128)S(1)}, u32[]{:S(2)}, u32[]{:S(2)}) collective-permute-start(f32[4,128]{1,0:T(4,128)S(1)} %add_add_fusion), channel_id=1, source_target_pairs={{0,1},{1,0},{2,3},{3,2},{4,5},{5,4},{6,7},{7,6},{8,9},{9,8},{10,11... | collective-permute-start | bytes 6152 | tf_op jit(solution)/shard_map/ppermute | solution.py:208
where the time goes:
time: 152 us; the launch traced here: 151 us
  waiting for transfers between devices  81 us (53%)
  starting transfers between devices  43.2 us (28%)
  Pallas kernels  23.2 us (15%)
  local copies, waits for them, and re-layouts  2.56 us (2%)
    all_to_all x3, waiting for transfers between devices, exchange(): lax.all_to_all(values, 'seq', split_axis=0, concat_axis=0, tiled=True)  62.3 us
    all_to_all x3, starting transfers between devices, exchange(): lax.all_to_all(values, 'seq', split_axis=0, concat_axis=0, tiled=True)  27.1 us
    ppermute x11, waiting for transfers between devices, flips(): lax.ppermute(values, axis, [(i, i ^ mask) for i in range(size)])  18.7 us
    ppermute x11, starting transfers between devices, flips(): lax.ppermute(values, axis, [(i, i ^ mask) for i in range(size)])  16.1 us
    pallas_call x1, Pallas kernels, per_device(): pl.pallas_call(spatial_bwd_kernel, name='spatial_bwd', grid=(XS,), out_sh...  8.57 us
    pallas_call x1, Pallas kernels, per_device(): pl.pallas_call(temporal_kernel, name='temporal', grid=(HEADS,), out_shape...  6.46 us
    pallas_call x1, Pallas kernels, per_device(): pl.pallas_call(pack_kernel, name='pack', grid=(XS // PACK_XS,), out_shape...  4.26 us
  transfers between devices with their start and end apart: 14, of which 9 were waited for; matrix products, arithmetic and copies ran while one was open for 0% of the time, Pallas kernels for 11%

commit v1 on v0

--- a/solution.py
+++ b/solution.py
@@ -95,16 +95,17 @@
     count = count_of(place_ref, seg_ref, counts_ref)
     live_keys = lax.broadcasted_iota(jnp.int32, (LIVE, LIVE), 0) < count
     for ref in (dq_ref, dk_ref, dv_ref):
-        ref[0, 0, LIVE:, :] = jnp.zeros((POS - LIVE, COLS), BF)
-    for h in range(HEADS):
+        ref[0, 0, LIVE:, :] = jnp.zeros((POS - LIVE, PACK_XS * COLS), BF)
+    for h in range(HEADS * PACK_XS):
         at = slice(h * HD, (h + 1) * HD)
+        x, to = h // HEADS, slice(h % HEADS * HD, (h % HEADS + 1) * HD)
         gq, gk = gains_ref[0:1, :], gains_ref[1:2, :]
         qh, qf = unit(q_ref[0, 0, :, at].astype(F32))
         kh, kf = unit(k_ref[0, 0, :, at].astype(F32))
         nq = (qh * gq).astype(BF)
         nk = (kh * gk).astype(BF)
         v = v_ref[0, 0, :, at]
-        g = g_ref[:, :, at].astype(F32).reshape(LIVE, HD).astype(BF)
+        g = g_ref[x * ZS : (x + 1) * ZS, :, to].astype(F32).reshape(LIVE, HD).astype(BF)
         w = spatial_weights(nq, nk, live_keys)
         dv = dot_nn(w.astype(BF), g)
         dw = dot_nt(v, g).astype(BF).astype(F32)
@@ -213,12 +214,8 @@
     return (values + one) + (two + both)
 
 
-def live_block():
-    return pl.BlockSpec((1, 1, LIVE, COLS), lambda i: (0, 0, 0, i))
-
-
-def full_block():
-    return pl.BlockSpec((1, 1, POS, COLS), lambda i: (0, 0, 0, i))
+def wide_block(rows):
+    return pl.BlockSpec((1, 1, rows, PACK_XS * COLS), lambda i: (0, 0, 0, i))
 
 
 def finish(packed, places):
@@ -254,7 +251,7 @@
         out_shape=jax.ShapeDtypeStruct((SEQ, 4, ROWS, COLS), BF),
         in_specs=[SMEM] * 3
         + [gains_spec]
-        + [pl.BlockSpec((1, 1, LIVE, PACK_XS * COLS), lambda i: (0, 0, 0, i))] * 6,
+        + [wide_block(LIVE)] * 6,
         out_specs=pl.BlockSpec((PACK_XS * ZS, 4, ROWS, COLS), lambda i: (i, 0, 0, 0)),
         compiler_params=WIDE,
         cost_estimate=cost(4 * LIVE * LIVE * FEAT, 10),
@@ -300,10 +297,13 @@
     dsq, dsk, dsv, gains_s = pl.pallas_call(
         spatial_bwd_kernel,
         name="spatial_bwd",
-        grid=(XS,),
+        grid=(XS // PACK_XS,),
         out_shape=[full, full, full, gg_shape],
-        in_specs=[SMEM] * 3 + [gains_spec] + [live_block()] * 3 + [pl.BlockSpec((ZS, ROWS, COLS), lambda i: (i, 0, 0))],
-        out_specs=[full_block()] * 3 + [gg_spec],
+        in_specs=[SMEM] * 3
+        + [gains_spec]
+        + [wide_block(LIVE)] * 3
+        + [pl.BlockSpec((PACK_XS * ZS, ROWS, COLS), lambda i: (i, 0, 0))],
+        out_specs=[wide_block(POS)] * 3 + [gg_spec],
         compiler_params=PARAMS,
         cost_estimate=cost(14 * LIVE * LIVE * FEAT, 8),
     )(*places, norm_gains, sq, sk, sv, dso)

time: 152 us -> 152 us (level)
  waiting for transfers between devices: 81 us -> 82.7 us
  transfers between devices with their start and end apart: 14 -> 14, of which waited for: 9 -> 9; matrix products, arithmetic and copies ran while one was open for 0% -> 0% of each run, Pallas kernels for 11% -> 10%
where the time goes in v1:
time: 152 us; the launch traced here: 151 us
  waiting for transfers between devices  82.7 us (54%)
  starting transfers between devices  42.2 us (28%)
  Pallas kernels  22.3 us (15%)
  local copies, waits for them, and re-layouts  2.56 us (2%)
    all_to_all x3, waiting for transfers between devices, exchange(): lax.all_to_all(values, 'seq', split_axis=0, concat_axis=0, tiled=True)  63.2 us
    all_to_all x3, starting transfers between devices, exchange(): lax.all_to_all(values, 'seq', split_axis=0, concat_axis=0, tiled=True)  26.2 us
    ppermute x11, waiting for transfers between devices, flips(): lax.ppermute(values, axis, [(i, i ^ mask) for i in range(size)])  19.5 us
    ppermute x11, starting transfers between devices, flips(): lax.ppermute(values, axis, [(i, i ^ mask) for i in range(size)])  16 us
    pallas_call x1, Pallas kernels, per_device(): pl.pallas_call(spatial_bwd_kernel, name='spatial_bwd', grid=(XS // PACK_X...  7.71 us
    pallas_call x1, Pallas kernels, per_device(): pl.pallas_call(temporal_kernel, name='temporal', grid=(HEADS,), out_shape...  6.46 us
    pallas_call x1, Pallas kernels, per_device(): pl.pallas_call(pack_kernel, name='pack', grid=(XS // PACK_XS,), out_shape...  4.26 us
  transfers between devices with their start and end apart: 14, of which 9 were waited for; matrix products, arithmetic and copies ran while one was open for 0% of the time, Pallas kernels for 10%

profile of v1, /device:TPU:12, one launch (start us, length us, event | category | flops | bytes accessed | tf_op | source)
XLA Modules:
  0.0 151.3 jit_solution(15836857463896896353)
XLA Ops:
  0.6 4.3 %pack.1 = bf16[32,4,24,384]{3,2,1,0:T(8,128)(2,1)} custom-call(s32[1]{0:T(128)} %bitcast.me_ref.place_ref, s32[1,32]{1,0:T(1,128)} %seg_ref.3, s32[1,4]{1,0:T(1,128)} %counts_ref.3, f32[4,128]{1,0:T(4,128)} %gains_ref.7, bf16[1,1,256,1536]{3,2,1,0:T(8,128)(2,1)} %tq_ref.1, bf16[1,1,256,1536]{3,2,1,0:T(8,128)(2,1)} %tk_ref.1, ...), custom_call_target="tpu_custom_call" | custom-call | flops 226492416 | bytes 5898240 | tf_op jit(solution)/shard_map/pack/pallas_call | solution.py:247
  4.9 0.0 copy-start.5
  4.9 0.0 copy-start.4
  4.9 11.7 %all-to-all-start = ((bf16[32,4,24,384]{3,2,1,0:T(8,128)(2,1)}), bf16[32,4,24,384]{3,2,1,0:T(8,128)(2,1)S(1)}, u32[]{:S(2)}, u32[]{:S(2)}) async-start(bf16[32,4,24,384]{3,2,1,0:T(8,128)(2,1)} %pack.1), calls=%async_computation | async-start | bytes 4718592 | tf_op jit(solution)/shard_map/all_to_all | solution.py:204
  16.7 0.0 copy-done.5
  16.7 0.1 broadcast_in_dim.2
  16.7 0.1 eq.30
  16.8 0.1 and_convert_fusion.mask_ref
  17.0 54.9 %all-to-all-done.got_ref.tq_ref.tk_ref.og_ref.so_ref = bf16[32,4,24,384]{3,2,1,0:T(8,128)(2,1)S(1)} async-done(((bf16[32,4,24,384]{3,2,1,0:T(8,128)(2,1)}), bf16[32,4,24,384]{3,2,1,0:T(8,128)(2,1)S(1)}, u32[]{:S(2)}, u32[]{:S(2)}) %all-to-all-start) | async-done | bytes 2359328 | tf_op jit(solution)/shard_map/all_to_all | solution.py:204
  71.9 0.0 copy-done.4
  71.9 2.3 %temporal_value.1 = bf16[32,24,384]{2,1,0:T(8,128)(2,1)} custom-call(f32[4,128]{1,0:T(4,128)S(1)} %copy-done.4, f32[256,256]{1,0:T(8,128)S(1)} %and_convert_fusion.mask_ref, bf16[32,4,24,384]{3,2,1,0:T(8,128)(2,1)S(1)} %all-to-all-done.got_ref.tq_ref.tk_ref.og_ref.so_ref), custom_call_target="tpu_custom_call" | custom-call | flops 301989888 | bytes 2359296 | tf_op jit(solution)/shard_map/temporal_value/pallas_call | solution.py:272
  74.3 7.0 %all-to-all-start.1 = ((bf16[32,24,384]{2,1,0:T(8,128)(2,1)}), bf16[32,24,384]{2,1,0:T(8,128)(2,1)}, u32[]{:S(2)}, u32[]{:S(2)}) async-start(bf16[32,24,384]{2,1,0:T(8,128)(2,1)} %temporal_value.1), calls=%async_computation.1 | async-start | bytes 1179648 | tf_op jit(solution)/shard_map/all_to_all | solution.py:204
  81.3 6.5 %temporal.1 = (bf16[32,3,24,384]{3,2,1,0:T(8,128)(2,1)S(1)}, f32[2,128]{1,0:T(2,128)S(1)}) custom-call(f32[4,128]{1,0:T(4,128)S(1)} %copy-done.4, f32[256,256]{1,0:T(8,128)S(1)} %and_convert_fusion.mask_ref, bf16[32,4,24,384]{3,2,1,0:T(8,128)(2,1)S(1)} %all-to-all-done.got_ref.tq_ref.tk_ref.og_ref.so_ref, ...), custom_call_target="tpu_custom_call" | custom-call | flops 905969664 | bytes 4128768 | tf_op jit(solution)/shard_map/temporal/pallas_call | solution.py:284
  87.8 0.0 copy-start.3
  87.8 1.2 copy-done.3
  89.0 8.2 %all-to-all-done.1.g_ref = bf16[32,24,384]{2,1,0:T(8,128)(2,1)} async-done(((bf16[32,24,384]{2,1,0:T(8,128)(2,1)}), bf16[32,24,384]{2,1,0:T(8,128)(2,1)}, u32[]{:S(2)}, u32[]{:S(2)}) %all-to-all-start.1) | async-done | bytes 589856 | tf_op jit(solution)/shard_map/all_to_all | solution.py:204
  97.3 7.4 %all-to-all-start.2 = ((bf16[32,3,24,384]{3,2,1,0:T(8,128)(2,1)}), bf16[32,3,24,384]{3,2,1,0:T(8,128)(2,1)S(1)}, u32[]{:S(2)}, u32[]{:S(2)}) async-start(bf16[32,3,24,384]{3,2,1,0:T(8,128)(2,1)} %copy-done.3), calls=%async_computation.2 | async-start | bytes 3538944 | tf_op jit(solution)/shard_map/all_to_all | solution.py:204
  104.7 0.0 copy-done
  104.7 0.0 copy-done.1
  104.7 0.0 copy-done.6
  104.7 0.0 copy-start.2
  104.7 1.1 copy-done.2
  105.8 7.7 %spatial_bwd.1 = (bf16[1,1,256,1536]{3,2,1,0:T(8,128)(2,1)}, bf16[1,1,256,1536]{3,2,1,0:T(8,128)(2,1)}, bf16[1,1,256,1536]{3,2,1,0:T(8,128)(2,1)}, f32[2,128]{1,0:T(2,128)S(1)}) custom-call(s32[1]{0:T(128)} %bitcast.me_ref.place_ref, s32[1,32]{1,0:T(1,128)S(1)} %copy-done.5, s32[1,4]{1,0:T(1,128)S(1)} %copy-done.6, f32[4,128]{1,0:T(4,128)S(1)} %copy-done.4, ...), custom_call_target="tpu_custom_call" | custom-call | flops 792723456 | bytes 4718592 | tf_op jit(solution)/shard_map/spatial_bwd/pallas_call | solution.py:297
  113.6 0.1 collective-permute-start
  113.7 1.1 collective-permute-done
  114.8 1.7 %collective-permute-start.3 = (f32[4,128]{1,0:T(4,128)S(1)}, f32[4,128]{1,0:T(4,128)S(1)}, u32[]{:S(2)}, u32[]{:S(2)}) collective-permute-start(f32[4,128]{1,0:T(4,128)S(1)} %fusion), channel_id=1, source_target_pairs={{0,192},{32,224},{64,128},{96,160},{128,64},{160,96},{192,0},{224,... | collective-permute-start | bytes 6152 | tf_op jit(solution)/shard_map/ppermute | solution.py:209
  116.5 0.9 collective-permute-start.2
  117.4 1.6 %collective-permute-start.1 = (f32[4,128]{1,0:T(4,128)S(1)}, f32[4,128]{1,0:T(4,128)S(1)}, u32[]{:S(2)}, u32[]{:S(2)}) collective-permute-start(f32[4,128]{1,0:T(4,128)S(1)} %fusion), channel_id=1, source_target_pairs={{0,64},{32,96},{64,0},{96,32},{128,192},{160,224},{192,128},{224,1... | collective-permute-start | bytes 6152 | tf_op jit(solution)/shard_map/ppermute | solution.py:209
  119.0 0.0 collective-permute-done.3
  119.0 2.6 %collective-permute-done.2 = f32[4,128]{1,0:T(4,128)S(1)} collective-permute-done((f32[4,128]{1,0:T(4,128)S(1)}, f32[4,128]{1,0:T(4,128)S(1)}, u32[]{:S(2)}, u32[]{:S(2)}) %collective-permute-start.2) | collective-permute-done | bytes 2080 | tf_op jit(solution)/shard_map/ppermute | solution.py:209
  121.6 0.0 collective-permute-done.1
  121.6 0.6 collective-permute-start.6
  122.2 2.7 %collective-permute-start.5 = (f32[4,128]{1,0:T(4,128)S(1)}, f32[4,128]{1,0:T(4,128)S(1)}, u32[]{:S(2)}, u32[]{:S(2)}) collective-permute-start(f32[4,128]{1,0:T(4,128)S(1)} %add_add_fusion.2), channel_id=1, source_target_pairs={{0,16},{1,17},{2,18},{3,19},{4,20},{5,21},{6,22},{7,23},{8,24},{9,... | collective-permute-start | bytes 6152 | tf_op jit(solution)/shard_map/ppermute | solution.py:209
  124.9 0.8 collective-permute-start.4
  125.8 0.0 collective-permute-done.6
  125.8 1.5 %collective-permute-done.5 = f32[4,128]{1,0:T(4,128)S(1)} collective-permute-done((f32[4,128]{1,0:T(4,128)S(1)}, f32[4,128]{1,0:T(4,128)S(1)}, u32[]{:S(2)}, u32[]{:S(2)}) %collective-permute-start.5) | collective-permute-done | bytes 2080 | tf_op jit(solution)/shard_map/ppermute | solution.py:209
  127.3 1.2 collective-permute-done.4
  128.5 3.6 %collective-permute-start.9 = (f32[4,128]{1,0:T(4,128)S(1)}, f32[4,128]{1,0:T(4,128)S(1)}, u32[]{:S(2)}, u32[]{:S(2)}) collective-permute-start(f32[4,128]{1,0:T(4,128)S(1)} %add_add_fusion.1), channel_id=1, source_target_pairs={{0,6},{1,7},{2,4},{3,5},{4,2},{5,3},{6,0},{7,1},{8,14},{9,15},{10,... | collective-permute-start | bytes 6152 | tf_op jit(solution)/shard_map/ppermute | solution.py:209
  132.1 2.5 %collective-permute-start.8 = (f32[4,128]{1,0:T(4,128)S(1)}, f32[4,128]{1,0:T(4,128)S(1)}, u32[]{:S(2)}, u32[]{:S(2)}) collective-permute-start(f32[4,128]{1,0:T(4,128)S(1)} %add_add_fusion.1), channel_id=1, source_target_pairs={{0,4},{1,5},{2,6},{3,7},{4,0},{5,1},{6,2},{7,3},{8,12},{9,13},{10,... | collective-permute-start | bytes 6152 | tf_op jit(solution)/shard_map/ppermute | solution.py:209
  134.6 0.4 collective-permute-start.7
  135.0 10.1 %collective-permute-done.9 = f32[4,128]{1,0:T(4,128)S(1)} collective-permute-done((f32[4,128]{1,0:T(4,128)S(1)}, f32[4,128]{1,0:T(4,128)S(1)}, u32[]{:S(2)}, u32[]{:S(2)}) %collective-permute-start.9) | collective-permute-done | bytes 2080 | tf_op jit(solution)/shard_map/ppermute | solution.py:209
  145.1 1.9 %collective-permute-done.8 = f32[4,128]{1,0:T(4,128)S(1)} collective-permute-done((f32[4,128]{1,0:T(4,128)S(1)}, f32[4,128]{1,0:T(4,128)S(1)}, u32[]{:S(2)}, u32[]{:S(2)}) %collective-permute-start.8) | collective-permute-done | bytes 2080 | tf_op jit(solution)/shard_map/ppermute | solution.py:209
  147.0 0.0 collective-permute-done.7
  147.0 0.0 all-to-all-done.2.refs_0_.refs_1_.refs_2_
  147.0 1.1 collective-permute-start.10
  148.1 1.5 %finish.1 = (bf16[1,1,256,1536]{3,2,1,0:T(8,128)(2,1)}, bf16[1,1,256,1536]{3,2,1,0:T(8,128)(2,1)}, bf16[1,1,256,1536]{3,2,1,0:T(8,128)(2,1)}) custom-call(bf16[32,3,24,384]{3,2,1,0:T(8,128)(2,1)S(1)} %all-to-all-done.2.refs_0_.refs_1_.refs_2_, bf16[32,3,24,384]{3,2,1,0:T(8,128)(2,1)S(1)} %all-to-all-done.2.refs_0_.refs_1_.refs_2_, ...), custom_call_target="tpu_custom_call" | custom-call | bytes 3538944 | tf_op jit(solution)/shard_map/finish/pallas_call | solution.py:223
  149.7 1.1 collective-permute-done.10
  150.7 0.6 add.58
  (9 shorter events, 0.0 us)
Async XLA Ops:
  4.9 11.8 %copy-start.5 = (s32[1,32]{1,0:T(1,128)S(1)}, s32[1,32]{1,0:T(1,128)}, u32[]{:S(2)}) copy-start(s32[1,32]{1,0:T(1,128)} %seg_ref.3) | copy-start | bytes 388
  4.9 67.0 %copy-start.4 = (f32[4,128]{1,0:T(4,128)S(1)}, f32[4,128]{1,0:T(4,128)}, u32[]{:S(2)}) copy-start(f32[4,128]{1,0:T(4,128)} %gains_ref.7) | copy-start | bytes 6148
  4.9 67.0 %all-to-all-start = ((bf16[32,4,24,384]{3,2,1,0:T(8,128)(2,1)}), bf16[32,4,24,384]{3,2,1,0:T(8,128)(2,1)S(1)}, u32[]{:S(2)}, u32[]{:S(2)}) async-start(bf16[32,4,24,384]{3,2,1,0:T(8,128)(2,1)} %pack.1), calls=%async_computation | async-start | bytes 4718592 | tf_op jit(solution)/shard_map/all_to_all | solution.py:204
  74.3 23.0 %all-to-all-start.1 = ((bf16[32,24,384]{2,1,0:T(8,128)(2,1)}), bf16[32,24,384]{2,1,0:T(8,128)(2,1)}, u32[]{:S(2)}, u32[]{:S(2)}) async-start(bf16[32,24,384]{2,1,0:T(8,128)(2,1)} %temporal_value.1), calls=%async_computation.1 | async-start | bytes 1179648 | tf_op jit(solution)/shard_map/all_to_all | solution.py:204
  87.8 1.3 copy-start.3
  89.0 15.6 %copy-start = (bf16[1,1,256,1536]{3,2,1,0:T(8,128)(2,1)S(1)}, bf16[1,1,256,1536]{3,2,1,0:T(8,128)(2,1)}, u32[]{:S(2)}) copy-start(bf16[1,1,256,1536]{3,2,1,0:T(8,128)(2,1)} %q_ref.3) | copy-start | bytes 2359300
  89.0 15.6 %copy-start.1 = (bf16[1,1,256,1536]{3,2,1,0:T(8,128)(2,1)S(1)}, bf16[1,1,256,1536]{3,2,1,0:T(8,128)(2,1)}, u32[]{:S(2)}) copy-start(bf16[1,1,256,1536]{3,2,1,0:T(8,128)(2,1)} %k_ref.3) | copy-start | bytes 2359300
  89.0 15.7 %copy-start.6 = (s32[1,4]{1,0:T(1,128)S(1)}, s32[1,4]{1,0:T(1,128)}, u32[]{:S(2)}) copy-start(s32[1,4]{1,0:T(1,128)} %counts_ref.3) | copy-start | bytes 52
  97.3 49.8 %all-to-all-start.2 = ((bf16[32,3,24,384]{3,2,1,0:T(8,128)(2,1)}), bf16[32,3,24,384]{3,2,1,0:T(8,128)(2,1)S(1)}, u32[]{:S(2)}, u32[]{:S(2)}) async-start(bf16[32,3,24,384]{3,2,1,0:T(8,128)(2,1)} %copy-done.3), calls=%async_computation.2 | async-start | bytes 3538944 | tf_op jit(solution)/shard_map/all_to_all | solution.py:204
  104.7 1.1 copy-start.2
  113.6 1.2 collective-permute-start
  114.8 4.2 %collective-permute-start.3 = (f32[4,128]{1,0:T(4,128)S(1)}, f32[4,128]{1,0:T(4,128)S(1)}, u32[]{:S(2)}, u32[]{:S(2)}) collective-permute-start(f32[4,128]{1,0:T(4,128)S(1)} %fusion), channel_id=1, source_target_pairs={{0,192},{32,224},{64,128},{96,160},{128,64},{160,96},{192,0},{224,... | collective-permute-start | bytes 6152 | tf_op jit(solution)/shard_map/ppermute | solution.py:209
  116.5 5.1 %collective-permute-start.2 = (f32[4,128]{1,0:T(4,128)S(1)}, f32[4,128]{1,0:T(4,128)S(1)}, u32[]{:S(2)}, u32[]{:S(2)}) collective-permute-start(f32[4,128]{1,0:T(4,128)S(1)} %fusion), channel_id=1, source_target_pairs={{0,128},{32,160},{64,192},{96,224},{128,0},{160,32},{192,64},{224,... | collective-permute-start | bytes 6152 | tf_op jit(solution)/shard_map/ppermute | solution.py:209
  117.4 4.2 %collective-permute-start.1 = (f32[4,128]{1,0:T(4,128)S(1)}, f32[4,128]{1,0:T(4,128)S(1)}, u32[]{:S(2)}, u32[]{:S(2)}) collective-permute-start(f32[4,128]{1,0:T(4,128)S(1)} %fusion), channel_id=1, source_target_pairs={{0,64},{32,96},{64,0},{96,32},{128,192},{160,224},{192,128},{224,1... | collective-permute-start | bytes 6152 | tf_op jit(solution)/shard_map/ppermute | solution.py:209
  121.6 4.2 %collective-permute-start.6 = (f32[4,128]{1,0:T(4,128)S(1)}, f32[4,128]{1,0:T(4,128)S(1)}, u32[]{:S(2)}, u32[]{:S(2)}) collective-permute-start(f32[4,128]{1,0:T(4,128)S(1)} %add_add_fusion.2), channel_id=1, source_target_pairs={{0,24},{1,25},{2,26},{3,27},{4,28},{5,29},{6,30},{7,31},{8,16},{9,... | collective-permute-start | bytes 6152 | tf_op jit(solution)/shard_map/ppermute | solution.py:209
  122.2 5.1 %collective-permute-start.5 = (f32[4,128]{1,0:T(4,128)S(1)}, f32[4,128]{1,0:T(4,128)S(1)}, u32[]{:S(2)}, u32[]{:S(2)}) collective-permute-start(f32[4,128]{1,0:T(4,128)S(1)} %add_add_fusion.2), channel_id=1, source_target_pairs={{0,16},{1,17},{2,18},{3,19},{4,20},{5,21},{6,22},{7,23},{8,24},{9,... | collective-permute-start | bytes 6152 | tf_op jit(solution)/shard_map/ppermute | solution.py:209
  124.9 3.6 %collective-permute-start.4 = (f32[4,128]{1,0:T(4,128)S(1)}, f32[4,128]{1,0:T(4,128)S(1)}, u32[]{:S(2)}, u32[]{:S(2)}) collective-permute-start(f32[4,128]{1,0:T(4,128)S(1)} %add_add_fusion.2), channel_id=1, source_target_pairs={{0,8},{1,9},{2,10},{3,11},{4,12},{5,13},{6,14},{7,15},{8,0},{9,1},... | collective-permute-start | bytes 6152 | tf_op jit(solution)/shard_map/ppermute | solution.py:209
  128.5 16.6 %collective-permute-start.9 = (f32[4,128]{1,0:T(4,128)S(1)}, f32[4,128]{1,0:T(4,128)S(1)}, u32[]{:S(2)}, u32[]{:S(2)}) collective-permute-start(f32[4,128]{1,0:T(4,128)S(1)} %add_add_fusion.1), channel_id=1, source_target_pairs={{0,6},{1,7},{2,4},{3,5},{4,2},{5,3},{6,0},{7,1},{8,14},{9,15},{10,... | collective-permute-start | bytes 6152 | tf_op jit(solution)/shard_map/ppermute | solution.py:209
  132.1 14.9 %collective-permute-start.8 = (f32[4,128]{1,0:T(4,128)S(1)}, f32[4,128]{1,0:T(4,128)S(1)}, u32[]{:S(2)}, u32[]{:S(2)}) collective-permute-start(f32[4,128]{1,0:T(4,128)S(1)} %add_add_fusion.1), channel_id=1, source_target_pairs={{0,4},{1,5},{2,6},{3,7},{4,0},{5,1},{6,2},{7,3},{8,12},{9,13},{10,... | collective-permute-start | bytes 6152 | tf_op jit(solution)/shard_map/ppermute | solution.py:209
  134.6 12.4 %collective-permute-start.7 = (f32[4,128]{1,0:T(4,128)S(1)}, f32[4,128]{1,0:T(4,128)S(1)}, u32[]{:S(2)}, u32[]{:S(2)}) collective-permute-start(f32[4,128]{1,0:T(4,128)S(1)} %add_add_fusion.1), channel_id=1, source_target_pairs={{0,2},{1,3},{2,0},{3,1},{4,6},{5,7},{6,4},{7,5},{8,10},{9,11},{10,... | collective-permute-start | bytes 6152 | tf_op jit(solution)/shard_map/ppermute | solution.py:209
  147.0 3.7 %collective-permute-start.10 = (f32[4,128]{1,0:T(4,128)S(1)}, f32[4,128]{1,0:T(4,128)S(1)}, u32[]{:S(2)}, u32[]{:S(2)}) collective-permute-start(f32[4,128]{1,0:T(4,128)S(1)} %add_add_fusion), channel_id=1, source_target_pairs={{0,1},{1,0},{2,3},{3,2},{4,5},{5,4},{6,7},{7,6},{8,9},{9,8},{10,11... | collective-permute-start | bytes 6152 | tf_op jit(solution)/shard_map/ppermute | solution.py:209

commit v2 on v1

--- a/solution.py
+++ b/solution.py
@@ -304,7 +304,7 @@
         + [wide_block(LIVE)] * 3
         + [pl.BlockSpec((PACK_XS * ZS, ROWS, COLS), lambda i: (i, 0, 0))],
         out_specs=[wide_block(POS)] * 3 + [gg_spec],
-        compiler_params=PARAMS,
+        compiler_params=WIDE,
         cost_estimate=cost(14 * LIVE * LIVE * FEAT, 8),
     )(*places, norm_gains, sq, sk, sv, dso)
     gains = jnp.concatenate([gains_s, gains_t], axis=0)

time: 152 us -> 152 us (level)
  transfers between devices with their start and end apart: 14 -> 14, of which waited for: 9 -> 9; matrix products, arithmetic and copies ran while one was open for 0% -> 1% of each run, Pallas kernels for 10% -> 11%
where the time goes in v2:
time: 152 us; the launch traced here: 151 us
  waiting for transfers between devices  82.8 us (54%)
  starting transfers between devices  41.7 us (27%)
  Pallas kernels  22.5 us (15%)
  other arithmetic  2.11 us (1%)
    all_to_all x3, waiting for transfers between devices, exchange(): lax.all_to_all(values, 'seq', split_axis=0, concat_axis=0, tiled=True)  63.5 us
    all_to_all x3, starting transfers between devices, exchange(): lax.all_to_all(values, 'seq', split_axis=0, concat_axis=0, tiled=True)  25.8 us
    ppermute x11, waiting for transfers between devices, flips(): lax.ppermute(values, axis, [(i, i ^ mask) for i in range(size)])  19.3 us
    ppermute x11, starting transfers between devices, flips(): lax.ppermute(values, axis, [(i, i ^ mask) for i in range(size)])  15.9 us
    pallas_call x1, Pallas kernels, per_device(): pl.pallas_call(spatial_bwd_kernel, name='spatial_bwd', grid=(XS // PACK_X...  7.95 us
    pallas_call x1, Pallas kernels, per_device(): pl.pallas_call(temporal_kernel, name='temporal', grid=(HEADS,), out_shape...  6.47 us
    pallas_call x1, Pallas kernels, per_device(): pl.pallas_call(pack_kernel, name='pack', grid=(XS // PACK_XS,), out_shape...  4.26 us
  transfers between devices with their start and end apart: 14, of which 9 were waited for; matrix products, arithmetic and copies ran while one was open for 1% of the time, Pallas kernels for 11%

profile of v2, /device:TPU:12, one launch (start us, length us, event | category | flops | bytes accessed | tf_op | source)
XLA Modules:
  0.0 151.3 jit_solution(6647988330947921555)
XLA Ops:
  0.6 4.3 %pack.1 = bf16[32,4,24,384]{3,2,1,0:T(8,128)(2,1)} custom-call(s32[1]{0:T(128)} %bitcast.me_ref.place_ref, s32[1,32]{1,0:T(1,128)} %seg_ref.3, s32[1,4]{1,0:T(1,128)} %counts_ref.3, f32[4,128]{1,0:T(4,128)} %gains_ref.7, bf16[1,1,256,1536]{3,2,1,0:T(8,128)(2,1)} %tq_ref.1, bf16[1,1,256,1536]{3,2,1,0:T(8,128)(2,1)} %tk_ref.1, ...), custom_call_target="tpu_custom_call" | custom-call | flops 226492416 | bytes 5898240 | tf_op jit(solution)/shard_map/pack/pallas_call | solution.py:247
  4.9 0.0 copy-start.3
  4.9 0.0 copy-start.1
  4.9 11.7 %all-to-all-start = ((bf16[32,4,24,384]{3,2,1,0:T(8,128)(2,1)}), bf16[32,4,24,384]{3,2,1,0:T(8,128)(2,1)S(1)}, u32[]{:S(2)}, u32[]{:S(2)}) async-start(bf16[32,4,24,384]{3,2,1,0:T(8,128)(2,1)} %pack.1), calls=%async_computation | async-start | bytes 4718592 | tf_op jit(solution)/shard_map/all_to_all | solution.py:204
  16.7 0.0 copy-done.3
  16.7 0.1 broadcast_in_dim.2
  16.7 0.1 eq.30
  16.8 0.1 and_convert_fusion.mask_ref
  17.0 54.9 %all-to-all-done.got_ref.tq_ref.tk_ref.og_ref.so_ref = bf16[32,4,24,384]{3,2,1,0:T(8,128)(2,1)S(1)} async-done(((bf16[32,4,24,384]{3,2,1,0:T(8,128)(2,1)}), bf16[32,4,24,384]{3,2,1,0:T(8,128)(2,1)S(1)}, u32[]{:S(2)}, u32[]{:S(2)}) %all-to-all-start) | async-done | bytes 2359328 | tf_op jit(solution)/shard_map/all_to_all | solution.py:204
  71.9 0.0 copy-done.1
  71.9 2.3 %temporal_value.1 = bf16[32,24,384]{2,1,0:T(8,128)(2,1)} custom-call(f32[4,128]{1,0:T(4,128)S(1)} %copy-done.1, f32[256,256]{1,0:T(8,128)S(1)} %and_convert_fusion.mask_ref, bf16[32,4,24,384]{3,2,1,0:T(8,128)(2,1)S(1)} %all-to-all-done.got_ref.tq_ref.tk_ref.og_ref.so_ref), custom_call_target="tpu_custom_call" | custom-call | flops 301989888 | bytes 2359296 | tf_op jit(solution)/shard_map/temporal_value/pallas_call | solution.py:272
  74.3 6.5 %all-to-all-start.1 = ((bf16[32,24,384]{2,1,0:T(8,128)(2,1)}), bf16[32,24,384]{2,1,0:T(8,128)(2,1)S(1)}, u32[]{:S(2)}, u32[]{:S(2)}) async-start(bf16[32,24,384]{2,1,0:T(8,128)(2,1)} %temporal_value.1), calls=%async_computation.1 | async-start | bytes 1179648 | tf_op jit(solution)/shard_map/all_to_all | solution.py:204
  80.8 6.5 %temporal.1 = (bf16[32,3,24,384]{3,2,1,0:T(8,128)(2,1)S(1)}, f32[2,128]{1,0:T(2,128)S(1)}) custom-call(f32[4,128]{1,0:T(4,128)S(1)} %copy-done.1, f32[256,256]{1,0:T(8,128)S(1)} %and_convert_fusion.mask_ref, bf16[32,4,24,384]{3,2,1,0:T(8,128)(2,1)S(1)} %all-to-all-done.got_ref.tq_ref.tk_ref.og_ref.so_ref, ...), custom_call_target="tpu_custom_call" | custom-call | flops 905969664 | bytes 4128768 | tf_op jit(solution)/shard_map/temporal/pallas_call | solution.py:284
  87.3 0.0 copy-start
  87.3 1.2 copy-done
  88.5 8.5 %all-to-all-done.1.g_ref = bf16[32,24,384]{2,1,0:T(8,128)(2,1)S(1)} async-done(((bf16[32,24,384]{2,1,0:T(8,128)(2,1)}), bf16[32,24,384]{2,1,0:T(8,128)(2,1)S(1)}, u32[]{:S(2)}, u32[]{:S(2)}) %all-to-all-start.1) | async-done | bytes 589856 | tf_op jit(solution)/shard_map/all_to_all | solution.py:204
  97.0 0.0 copy-start.2
  97.0 7.5 %all-to-all-start.2 = ((bf16[32,3,24,384]{3,2,1,0:T(8,128)(2,1)}), bf16[32,3,24,384]{3,2,1,0:T(8,128)(2,1)S(1)}, u32[]{:S(2)}, u32[]{:S(2)}) async-start(bf16[32,3,24,384]{3,2,1,0:T(8,128)(2,1)} %copy-done), calls=%async_computation.2 | async-start | bytes 3538944 | tf_op jit(solution)/shard_map/all_to_all | solution.py:204
  104.6 0.0 copy-done.2
  104.6 8.0 %spatial_bwd.1 = (bf16[1,1,256,1536]{3,2,1,0:T(8,128)(2,1)}, bf16[1,1,256,1536]{3,2,1,0:T(8,128)(2,1)}, bf16[1,1,256,1536]{3,2,1,0:T(8,128)(2,1)}, f32[2,128]{1,0:T(2,128)}) custom-call(s32[1]{0:T(128)} %bitcast.me_ref.place_ref, s32[1,32]{1,0:T(1,128)} %seg_ref.3, s32[1,4]{1,0:T(1,128)} %counts_ref.3, f32[4,128]{1,0:T(4,128)} %gains_ref.7, ...), custom_call_target="tpu_custom_call" | custom-call | flops 792723456 | bytes 4718592 | tf_op jit(solution)/shard_map/spatial_bwd/pallas_call | solution.py:297
  112.5 0.7 pad_maximum_fusion
  113.2 0.0 collective-permute-start
  113.2 1.2 collective-permute-done
  114.4 0.7 fusion
  115.1 1.6 %collective-permute-start.3 = (f32[4,128]{1,0:T(4,128)S(1)}, f32[4,128]{1,0:T(4,128)S(1)}, u32[]{:S(2)}, u32[]{:S(2)}) collective-permute-start(f32[4,128]{1,0:T(4,128)S(1)} %fusion), channel_id=1, source_target_pairs={{0,192},{32,224},{64,128},{96,160},{128,64},{160,96},{192,0},{224,... | collective-permute-start | bytes 6152 | tf_op jit(solution)/shard_map/ppermute | solution.py:209
  116.6 0.9 collective-permute-start.2
  117.6 1.6 %collective-permute-start.1 = (f32[4,128]{1,0:T(4,128)S(1)}, f32[4,128]{1,0:T(4,128)S(1)}, u32[]{:S(2)}, u32[]{:S(2)}) collective-permute-start(f32[4,128]{1,0:T(4,128)S(1)} %fusion), channel_id=1, source_target_pairs={{0,64},{32,96},{64,0},{96,32},{128,192},{160,224},{192,128},{224,1... | collective-permute-start | bytes 6152 | tf_op jit(solution)/shard_map/ppermute | solution.py:209
  119.2 0.0 collective-permute-done.3
  119.2 2.6 %collective-permute-done.2 = f32[4,128]{1,0:T(4,128)S(1)} collective-permute-done((f32[4,128]{1,0:T(4,128)S(1)}, f32[4,128]{1,0:T(4,128)S(1)}, u32[]{:S(2)}, u32[]{:S(2)}) %collective-permute-start.2) | collective-permute-done | bytes 2080 | tf_op jit(solution)/shard_map/ppermute | solution.py:209
  121.7 0.0 collective-permute-done.1
  121.7 0.6 collective-permute-start.6
  122.4 2.7 %collective-permute-start.5 = (f32[4,128]{1,0:T(4,128)S(1)}, f32[4,128]{1,0:T(4,128)S(1)}, u32[]{:S(2)}, u32[]{:S(2)}) collective-permute-start(f32[4,128]{1,0:T(4,128)S(1)} %add_add_fusion.2), channel_id=1, source_target_pairs={{0,16},{1,17},{2,18},{3,19},{4,20},{5,21},{6,22},{7,23},{8,24},{9,... | collective-permute-start | bytes 6152 | tf_op jit(solution)/shard_map/ppermute | solution.py:209
  125.1 0.8 collective-permute-start.4
  125.9 0.0 collective-permute-done.6
  125.9 1.5 %collective-permute-done.5 = f32[4,128]{1,0:T(4,128)S(1)} collective-permute-done((f32[4,128]{1,0:T(4,128)S(1)}, f32[4,128]{1,0:T(4,128)S(1)}, u32[]{:S(2)}, u32[]{:S(2)}) %collective-permute-start.5) | collective-permute-done | bytes 2080 | tf_op jit(solution)/shard_map/ppermute | solution.py:209
  127.5 1.2 collective-permute-done.4
  128.7 3.6 %collective-permute-start.9 = (f32[4,128]{1,0:T(4,128)S(1)}, f32[4,128]{1,0:T(4,128)S(1)}, u32[]{:S(2)}, u32[]{:S(2)}) collective-permute-start(f32[4,128]{1,0:T(4,128)S(1)} %add_add_fusion.1), channel_id=1, source_target_pairs={{0,6},{1,7},{2,4},{3,5},{4,2},{5,3},{6,0},{7,1},{8,14},{9,15},{10,... | collective-permute-start | bytes 6152 | tf_op jit(solution)/shard_map/ppermute | solution.py:209
  132.3 2.5 %collective-permute-start.8 = (f32[4,128]{1,0:T(4,128)S(1)}, f32[4,128]{1,0:T(4,128)S(1)}, u32[]{:S(2)}, u32[]{:S(2)}) collective-permute-start(f32[4,128]{1,0:T(4,128)S(1)} %add_add_fusion.1), channel_id=1, source_target_pairs={{0,4},{1,5},{2,6},{3,7},{4,0},{5,1},{6,2},{7,3},{8,12},{9,13},{10,... | collective-permute-start | bytes 6152 | tf_op jit(solution)/shard_map/ppermute | solution.py:209
  134.8 0.4 collective-permute-start.7
  135.2 9.9 %collective-permute-done.9 = f32[4,128]{1,0:T(4,128)S(1)} collective-permute-done((f32[4,128]{1,0:T(4,128)S(1)}, f32[4,128]{1,0:T(4,128)S(1)}, u32[]{:S(2)}, u32[]{:S(2)}) %collective-permute-start.9) | collective-permute-done | bytes 2080 | tf_op jit(solution)/shard_map/ppermute | solution.py:209
  145.1 1.9 %collective-permute-done.8 = f32[4,128]{1,0:T(4,128)S(1)} collective-permute-done((f32[4,128]{1,0:T(4,128)S(1)}, f32[4,128]{1,0:T(4,128)S(1)}, u32[]{:S(2)}, u32[]{:S(2)}) %collective-permute-start.8) | collective-permute-done | bytes 2080 | tf_op jit(solution)/shard_map/ppermute | solution.py:209
  147.0 0.0 collective-permute-done.7
  147.0 0.0 all-to-all-done.2.refs_0_.refs_1_.refs_2_
  147.1 1.2 collective-permute-start.10
  148.2 1.5 %finish.1 = (bf16[1,1,256,1536]{3,2,1,0:T(8,128)(2,1)}, bf16[1,1,256,1536]{3,2,1,0:T(8,128)(2,1)}, bf16[1,1,256,1536]{3,2,1,0:T(8,128)(2,1)}) custom-call(bf16[32,3,24,384]{3,2,1,0:T(8,128)(2,1)S(1)} %all-to-all-done.2.refs_0_.refs_1_.refs_2_, bf16[32,3,24,384]{3,2,1,0:T(8,128)(2,1)S(1)} %all-to-all-done.2.refs_0_.refs_1_.refs_2_, ...), custom_call_target="tpu_custom_call" | custom-call | bytes 3538944 | tf_op jit(solution)/shard_map/finish/pallas_call | solution.py:223
  149.7 1.0 collective-permute-done.10
  150.7 0.6 add.58
  (4 shorter events, 0.0 us)
Async XLA Ops:
  4.9 11.8 %copy-start.3 = (s32[1,32]{1,0:T(1,128)S(1)}, s32[1,32]{1,0:T(1,128)}, u32[]{:S(2)}) copy-start(s32[1,32]{1,0:T(1,128)} %seg_ref.3) | copy-start | bytes 388
  4.9 67.0 %copy-start.1 = (f32[4,128]{1,0:T(4,128)S(1)}, f32[4,128]{1,0:T(4,128)}, u32[]{:S(2)}) copy-start(f32[4,128]{1,0:T(4,128)} %gains_ref.7) | copy-start | bytes 6148
  4.9 67.0 %all-to-all-start = ((bf16[32,4,24,384]{3,2,1,0:T(8,128)(2,1)}), bf16[32,4,24,384]{3,2,1,0:T(8,128)(2,1)S(1)}, u32[]{:S(2)}, u32[]{:S(2)}) async-start(bf16[32,4,24,384]{3,2,1,0:T(8,128)(2,1)} %pack.1), calls=%async_computation | async-start | bytes 4718592 | tf_op jit(solution)/shard_map/all_to_all | solution.py:204
  74.3 22.8 %all-to-all-start.1 = ((bf16[32,24,384]{2,1,0:T(8,128)(2,1)}), bf16[32,24,384]{2,1,0:T(8,128)(2,1)S(1)}, u32[]{:S(2)}, u32[]{:S(2)}) async-start(bf16[32,24,384]{2,1,0:T(8,128)(2,1)} %temporal_value.1), calls=%async_computation.1 | async-start | bytes 1179648 | tf_op jit(solution)/shard_map/all_to_all | solution.py:204
  87.3 1.2 copy-start
  97.0 7.5 %copy-start.2 = (bf16[32,24,384]{2,1,0:T(8,128)(2,1)}, bf16[32,24,384]{2,1,0:T(8,128)(2,1)S(1)}, u32[]{:S(2)}) copy-start(bf16[32,24,384]{2,1,0:T(8,128)(2,1)S(1)} %all-to-all-done.1.g_ref) | copy-start | bytes 1769476
  97.0 50.0 %all-to-all-start.2 = ((bf16[32,3,24,384]{3,2,1,0:T(8,128)(2,1)}), bf16[32,3,24,384]{3,2,1,0:T(8,128)(2,1)S(1)}, u32[]{:S(2)}, u32[]{:S(2)}) async-start(bf16[32,3,24,384]{3,2,1,0:T(8,128)(2,1)} %copy-done), calls=%async_computation.2 | async-start | bytes 3538944 | tf_op jit(solution)/shard_map/all_to_all | solution.py:204
  113.2 1.2 collective-permute-start
  115.1 4.1 %collective-permute-start.3 = (f32[4,128]{1,0:T(4,128)S(1)}, f32[4,128]{1,0:T(4,128)S(1)}, u32[]{:S(2)}, u32[]{:S(2)}) collective-permute-start(f32[4,128]{1,0:T(4,128)S(1)} %fusion), channel_id=1, source_target_pairs={{0,192},{32,224},{64,128},{96,160},{128,64},{160,96},{192,0},{224,... | collective-permute-start | bytes 6152 | tf_op jit(solution)/shard_map/ppermute | solution.py:209
  116.6 5.1 %collective-permute-start.2 = (f32[4,128]{1,0:T(4,128)S(1)}, f32[4,128]{1,0:T(4,128)S(1)}, u32[]{:S(2)}, u32[]{:S(2)}) collective-permute-start(f32[4,128]{1,0:T(4,128)S(1)} %fusion), channel_id=1, source_target_pairs={{0,128},{32,160},{64,192},{96,224},{128,0},{160,32},{192,64},{224,... | collective-permute-start | bytes 6152 | tf_op jit(solution)/shard_map/ppermute | solution.py:209
  117.6 4.2 %collective-permute-start.1 = (f32[4,128]{1,0:T(4,128)S(1)}, f32[4,128]{1,0:T(4,128)S(1)}, u32[]{:S(2)}, u32[]{:S(2)}) collective-permute-start(f32[4,128]{1,0:T(4,128)S(1)} %fusion), channel_id=1, source_target_pairs={{0,64},{32,96},{64,0},{96,32},{128,192},{160,224},{192,128},{224,1... | collective-permute-start | bytes 6152 | tf_op jit(solution)/shard_map/ppermute | solution.py:209
  121.7 4.2 %collective-permute-start.6 = (f32[4,128]{1,0:T(4,128)S(1)}, f32[4,128]{1,0:T(4,128)S(1)}, u32[]{:S(2)}, u32[]{:S(2)}) collective-permute-start(f32[4,128]{1,0:T(4,128)S(1)} %add_add_fusion.2), channel_id=1, source_target_pairs={{0,24},{1,25},{2,26},{3,27},{4,28},{5,29},{6,30},{7,31},{8,16},{9,... | collective-permute-start | bytes 6152 | tf_op jit(solution)/shard_map/ppermute | solution.py:209
  122.4 5.1 %collective-permute-start.5 = (f32[4,128]{1,0:T(4,128)S(1)}, f32[4,128]{1,0:T(4,128)S(1)}, u32[]{:S(2)}, u32[]{:S(2)}) collective-permute-start(f32[4,128]{1,0:T(4,128)S(1)} %add_add_fusion.2), channel_id=1, source_target_pairs={{0,16},{1,17},{2,18},{3,19},{4,20},{5,21},{6,22},{7,23},{8,24},{9,... | collective-permute-start | bytes 6152 | tf_op jit(solution)/shard_map/ppermute | solution.py:209
  125.1 3.6 %collective-permute-start.4 = (f32[4,128]{1,0:T(4,128)S(1)}, f32[4,128]{1,0:T(4,128)S(1)}, u32[]{:S(2)}, u32[]{:S(2)}) collective-permute-start(f32[4,128]{1,0:T(4,128)S(1)} %add_add_fusion.2), channel_id=1, source_target_pairs={{0,8},{1,9},{2,10},{3,11},{4,12},{5,13},{6,14},{7,15},{8,0},{9,1},... | collective-permute-start | bytes 6152 | tf_op jit(solution)/shard_map/ppermute | solution.py:209
  128.7 16.4 %collective-permute-start.9 = (f32[4,128]{1,0:T(4,128)S(1)}, f32[4,128]{1,0:T(4,128)S(1)}, u32[]{:S(2)}, u32[]{:S(2)}) collective-permute-start(f32[4,128]{1,0:T(4,128)S(1)} %add_add_fusion.1), channel_id=1, source_target_pairs={{0,6},{1,7},{2,4},{3,5},{4,2},{5,3},{6,0},{7,1},{8,14},{9,15},{10,... | collective-permute-start | bytes 6152 | tf_op jit(solution)/shard_map/ppermute | solution.py:209
  132.3 14.7 %collective-permute-start.8 = (f32[4,128]{1,0:T(4,128)S(1)}, f32[4,128]{1,0:T(4,128)S(1)}, u32[]{:S(2)}, u32[]{:S(2)}) collective-permute-start(f32[4,128]{1,0:T(4,128)S(1)} %add_add_fusion.1), channel_id=1, source_target_pairs={{0,4},{1,5},{2,6},{3,7},{4,0},{5,1},{6,2},{7,3},{8,12},{9,13},{10,... | collective-permute-start | bytes 6152 | tf_op jit(solution)/shard_map/ppermute | solution.py:209
  134.8 12.2 %collective-permute-start.7 = (f32[4,128]{1,0:T(4,128)S(1)}, f32[4,128]{1,0:T(4,128)S(1)}, u32[]{:S(2)}, u32[]{:S(2)}) collective-permute-start(f32[4,128]{1,0:T(4,128)S(1)} %add_add_fusion.1), channel_id=1, source_target_pairs={{0,2},{1,3},{2,0},{3,1},{4,6},{5,7},{6,4},{7,5},{8,10},{9,11},{10,... | collective-permute-start | bytes 6152 | tf_op jit(solution)/shard_map/ppermute | solution.py:209
  147.1 3.7 %collective-permute-start.10 = (f32[4,128]{1,0:T(4,128)S(1)}, f32[4,128]{1,0:T(4,128)S(1)}, u32[]{:S(2)}, u32[]{:S(2)}) collective-permute-start(f32[4,128]{1,0:T(4,128)S(1)} %add_add_fusion), channel_id=1, source_target_pairs={{0,1},{1,0},{2,3},{3,2},{4,5},{5,4},{6,7},{7,6},{8,9},{9,8},{10,11... | collective-permute-start | bytes 6152 | tf_op jit(solution)/shard_map/ppermute | solution.py:209
